TPU v7x, 128 devices: a whole 4x4x4 slice. The times are simulated.
128 devices in a mesh: dp: 64 (over x_hi, y, z, core), mp: 2 (over x_lo).
Axes of the slice: x: 4 (x_hi: 2, x_lo: 2; x = x_hi * 2 + x_lo), y: 4, z: 4, core: 2. Of those that a mesh axis runs over, the one named last changes fastest.
Arguments:
- image_emb: bfloat16 [8192, 1152], P('dp', 'mp'), may hold values from -0.1875 to 0.1875
- caption_emb: bfloat16 [12288, 1152], P('dp', 'mp'), may hold values from -0.1875 to 0.1875
- caption_count: int32 [8192], P('dp'), may hold values from 1 to 5, as said below
- caption_owner: int32 [12288], P('dp'), may hold values from 0 to 63, as said below
- pair_image: int32 [16384], P('dp'), may hold values from -1 to 127, as said below
Outputs:
- image_grad: bfloat16 [8192, 1152], P('dp', 'mp')
- caption_grad: bfloat16 [12288, 1152], P('dp', 'mp')
Inputs may be any that keep to these rules, and one draw needn't show every extreme that they name: `caption_owner`: each loader sends either 2 or 4 of its rows to each owner; some owner receives 4 rows from every loader. `pair_image`: slot s * 4 + r of owner o names an image exactly when loader s sends more than r rows to o, and holds -1 otherwise; every image of the owner is named at least once. caption_count[i] is the number of slots that name image i.
All inputs are finite; a program needn't handle non-finite values.
Results may differ from a plain program's by a relative error of at most 0.0013.
The roundings to bfloat16 on the way count: a program that leaves them out, or rounds other values in their place, can miss the bound.
Values may be sent and summed in bfloat16 or wider, within the bound.
No kernel may reach another device: no remote copies, remote signals or barrier semaphores. Data moves between devices by JAX's collectives and lax.ppermute only.
A program may use at most 192 MiB of HBM per device.

v0:
```python
import jax
import jax.numpy as jnp
from jax import lax
from jax.sharding import PartitionSpec as P

logit_scale = 10.0
logit_bias = -2.0


def cross_rows(left, right):
    return lax.dot_general(
        left, right, (((1,), (1,)), ((), ())), preferred_element_type=jnp.float32
    )


def down_rows(left, right):
    return lax.dot_general(
        left, right, (((0,), (0,)), ((), ())), preferred_element_type=jnp.float32
    )


def make_coefficient(products, positive, inverse_count):
    logits = logit_scale * products + logit_bias
    weight = 1.0 + positive * (inverse_count - 1.0)
    return (logit_scale * weight * (jax.nn.sigmoid(logits) - positive)).astype(jnp.bfloat16)


def body(image_emb, caption_emb, caption_count, caption_owner, pair_image):
    groups = lax.axis_size("dp")
    slot_count = pair_image.shape[0]
    load_count = caption_owner.shape[0]
    image_count = image_emb.shape[0]
    half_width = image_emb.shape[1]
    per_owner = slot_count // groups
    column = lax.axis_index("mp") * half_width
    holder = lax.axis_index("dp")
    positions = jnp.arange(load_count, dtype=jnp.int32)
    earlier = positions[None, :] < positions[:, None]
    same_owner = caption_owner[:, None] == caption_owner[None, :]
    rank_index = jnp.sum((same_owner & earlier).astype(jnp.int32), axis=1)
    slot_index = caption_owner * per_owner + rank_index
    placing = (jnp.arange(slot_count, dtype=jnp.int32)[:, None] == slot_index[None, :]).astype(
        jnp.bfloat16
    )
    outgoing = jnp.dot(placing, caption_emb, preferred_element_type=jnp.float32).astype(
        jnp.bfloat16
    )
    owned_rows = lax.all_to_all(outgoing, "dp", split_axis=0, concat_axis=0, tiled=True)
    images_wide, captions_wide = (
        lax.all_gather(image_emb, "mp", axis=1, tiled=True),
        lax.all_gather(owned_rows, "mp", axis=1, tiled=True),
    )
    local_rows = jnp.arange(image_count, dtype=jnp.int32)
    inverse_count = 1.0 / caption_count.astype(jnp.float32)
    slot_global = jnp.where(pair_image >= 0, holder * image_count + pair_image, -1)
    own_positive = (pair_image[None, :] == local_rows[:, None]).astype(jnp.float32)
    slot_inverse = jnp.sum(own_positive * inverse_count[:, None], axis=0)
    piece = lax.all_gather(images_wide, "dp", axis=0, tiled=True)
    count = piece.shape[0]
    piece_rows = jnp.arange(count, dtype=jnp.int32)
    positive = (piece_rows[:, None] == slot_global[None, :]).astype(jnp.float32)
    coefficient = make_coefficient(
        cross_rows(piece, captions_wide), positive, slot_inverse[None, :]
    )
    piece_half = lax.dynamic_slice_in_dim(piece, column, half_width, 1)
    text_total = down_rows(coefficient, piece_half)
    image_terms = jnp.dot(coefficient, owned_rows, preferred_element_type=jnp.float32)
    text_total, image_terms = (text_total, image_terms)
    image_total = lax.psum_scatter(image_terms, "dp", scatter_dimension=0, tiled=True)
    returned = lax.all_to_all(
        text_total.astype(jnp.bfloat16), "dp", split_axis=0, concat_axis=0, tiled=True
    )
    caption_grad = jnp.take(returned, slot_index, axis=0)
    return (image_total.astype(jnp.bfloat16), caption_grad)


def solution(mesh):
    in_specs = (P("dp", "mp"), P("dp", "mp"), P("dp"), P("dp"), P("dp"))
    out_specs = (P("dp", "mp"), P("dp", "mp"))
    return jax.shard_map(body, mesh=mesh, in_specs=in_specs, out_specs=out_specs, check_vma=False)
```

profile of v0, /device:TPU:0, one launch (start us, length us, event | category | flops | bytes accessed | tf_op | source)
XLA Modules:
  0.0 409.5 jit_solution(10440924156195011961)
XLA Ops:
  7.2 0.0 copy-start
  7.2 0.0 all-gather.2.cloned.1.call-start
  7.2 8.1 %all_gather.10 = bf16[128,1152]{0,1:T(8,128)(2,1)} all-gather(bf16[128,576]{0,1:T(8,128)(2,1)} %param.5), channel_id=1, replica_groups=mesh['dp'=64,'mp'=2] {'mp'}, dimensions={1}, use_global_device_ids=true | all-gather | bytes 442368 | tf_op jit(solution)/shard_map/all_gather | solution.py:50
  15.3 0.0 all-gather.2.cloned.1.call-update
  15.3 0.9 convert_reduce_fusion
  16.3 0.7 compare_and_fusion
  17.0 0.0 copy-done
  17.0 0.3 convolution_convert_fusion
  17.3 0.2 copy.13
  17.5 0.8 all_to_all.16
  18.3 11.1 %all-to-all-start = ((bf16[64,4,576]{2,1,0:T(4,128)(2,1)}), bf16[64,4,576]{2,1,0:T(4,128)(2,1)S(1)}, u32[]{:S(2)}, u32[]{:S(2)}) async-start(bf16[64,4,576]{2,1,0:T(4,128)(2,1)} %all_to_all.16), calls=%async_computation | async-start | bytes 655360 | tf_op jit(solution)/shard_map/all_to_all | solution.py:48
  29.4 0.0 reduce-scatter.2.cloned.1.call-start
  29.5 0.7 convert_divide_fusion
  30.1 0.7 compare_select_fusion.1
  30.8 0.8 select_reduce_fusion
  31.6 11.4 %all-to-all-done = bf16[64,4,576]{2,1,0:T(4,128)(2,1)S(1)} async-done(((bf16[64,4,576]{2,1,0:T(4,128)(2,1)}), bf16[64,4,576]{2,1,0:T(4,128)(2,1)S(1)}, u32[]{:S(2)}, u32[]{:S(2)}) %all-to-all-start) | async-done | bytes 294944 | tf_op jit(solution)/shard_map/all_to_all | solution.py:48
  43.0 0.2 all_to_all.18
  43.2 0.2 copy.14
  43.4 9.7 %all_gather.9 = bf16[256,1152]{0,1:T(8,128)(2,1)S(1)} all-gather(bf16[256,576]{0,1:T(8,128)(2,1)S(1)} %copy.14), channel_id=1, replica_groups=mesh['dp'=64,'mp'=2] {'mp'}, dimensions={1}, use_global_device_ids=true | all-gather | bytes 884736 | tf_op jit(solution)/shard_map/all_gather | solution.py:51
  53.1 114.2 %all-gather.2.cloned.1.call-done = bf16[8192,1152]{0,1:T(8,128)(2,1)} async-done(((bf16[128,1152]{0,1:T(8,128)(2,1)}), bf16[8192,1152]{0,1:T(8,128)(2,1)}) %all-gather.2.cloned.1.call-update) | async-done | bytes 18874384 | tf_op jit(solution)/shard_map/all_gather | solution.py:58
  167.3 13.1 %fusion.8 = bf16[8192,256]{0,1:T(8,128)(2,1)S(1)} fusion(bf16[256,1152]{0,1:T(8,128)(2,1)S(1)} %all_gather.9, bf16[8192,1152]{0,1:T(8,128)(2,1)} %all-gather.2.cloned.1.call-done, f32[256]{0:T(256)S(1)} %broadcast_add_fusion, s32[256]{0:T(256)S(1)} %compare_select_fusion.1), kind=kOutput, calls=%fused_computation.10 | convolution fusion | flops 4859101184 | bytes 23660544 | tf_op jit(solution)/shard_map/dot_general | solution.py:11
  180.4 0.0 copy-start.1
  180.4 1.9 copy-done.1
  182.3 8.0 %fusion.17 = f32[8192,576]{0,1:T(8,128)} fusion(bf16[8192,256]{0,1:T(8,128)(2,1)S(1)} %fusion.8, bf16[256,576]{1,0:T(8,128)(2,1)S(1)} %all_to_all.18), kind=kOutput, calls=%fused_computation.32 | convolution fusion | flops 2415919104 | bytes 23363584 | tf_op jit(solution)/shard_map/dot_general | solution.py:67
  190.3 0.0 reduce-scatter.2.cloned.1.call-update
  190.3 7.6 %fusion.11 = bf16[256,576]{0,1:T(8,128)(2,1)S(1)} fusion(bf16[8192,256]{0,1:T(8,128)(2,1)} %copy-done.1, bf16[8192,1152]{0,1:T(8,128)(2,1)} %all-gather.2.cloned.1.call-done, s32[]{:T(128)S(6)} %select_n.18), kind=kOutput, calls=%fused_computation.15 | convolution fusion | flops 2416066560 | bytes 13926404 | tf_op jit(solution)/shard_map/dot_general | solution.py:17
  197.9 0.2 copy.15
  198.1 0.8 all_to_all.19
  198.9 5.5 %all-to-all-start.1 = ((bf16[64,4,576]{2,1,0:T(4,128)(2,1)}), bf16[64,4,576]{2,1,0:T(4,128)(2,1)S(1)}, u32[]{:S(2)}, u32[]{:S(2)}) async-start(bf16[64,4,576]{2,1,0:T(4,128)(2,1)} %all_to_all.19), calls=%async_computation.2 | async-start | bytes 655360 | tf_op jit(solution)/shard_map/all_to_all | solution.py:70
  204.5 11.8 %all-to-all-done.1 = bf16[64,4,576]{2,1,0:T(4,128)(2,1)S(1)} async-done(((bf16[64,4,576]{2,1,0:T(4,128)(2,1)}), bf16[64,4,576]{2,1,0:T(4,128)(2,1)S(1)}, u32[]{:S(2)}, u32[]{:S(2)}) %all-to-all-start.1) | async-done | bytes 294944 | tf_op jit(solution)/shard_map/all_to_all | solution.py:70
  216.2 0.2 all_to_all.21
  216.4 1.0 gather_fusion
  217.4 0.8 broadcast_select_fusion
  218.2 182.7 %reduce-scatter.2.cloned.1.call-done = f32[128,576]{0,1:T(8,128)} async-done(((f32[8192,576]{0,1:T(8,128)}), f32[128,576]{0,1:T(8,128)}) %reduce-scatter.2.cloned.1.call-update) | async-done | bytes 294928 | tf_op jit(solution)/shard_map/reduce_scatter | solution.py:69
  401.0 1.6 convert_element_type.28
  (3 shorter events, 0.0 us)
Async XLA Ops:
  7.2 9.8 %copy-start = (bf16[192,576]{1,0:T(8,128)(2,1)S(1)}, bf16[192,576]{1,0:T(8,128)(2,1)}, u32[]{:S(2)}) copy-start(bf16[192,576]{1,0:T(8,128)(2,1)} %param.6) | copy-start | bytes 663556
  7.2 160.1 %all-gather.2.cloned.1.call-start = ((), (), s32[]{:S(2)}) async-start(), calls=%async_computation.3 | async-start | bytes 19169280 | tf_op jit(solution)/shard_map/all_gather | solution.py:58
  18.3 24.7 %all-to-all-start = ((bf16[64,4,576]{2,1,0:T(4,128)(2,1)}), bf16[64,4,576]{2,1,0:T(4,128)(2,1)S(1)}, u32[]{:S(2)}, u32[]{:S(2)}) async-start(bf16[64,4,576]{2,1,0:T(4,128)(2,1)} %all_to_all.16), calls=%async_computation | async-start | bytes 655360 | tf_op jit(solution)/shard_map/all_to_all | solution.py:48
  29.4 371.5 %reduce-scatter.2.cloned.1.call-start = ((), (), s32[]{:S(2)}) async-start(), calls=%async_computation.4 | async-start | bytes 19169280 | tf_op jit(solution)/shard_map/reduce_scatter | solution.py:69
  180.4 2.0 copy-start.1
  198.9 17.3 %all-to-all-start.1 = ((bf16[64,4,576]{2,1,0:T(4,128)(2,1)}), bf16[64,4,576]{2,1,0:T(4,128)(2,1)S(1)}, u32[]{:S(2)}, u32[]{:S(2)}) async-start(bf16[64,4,576]{2,1,0:T(4,128)(2,1)} %all_to_all.19), calls=%async_computation.2 | async-start | bytes 655360 | tf_op jit(solution)/shard_map/all_to_all | solution.py:70
Sparse Core Ops, SparseCore 0:
  15.5 151.7 all-gather.1
  190.4 210.4 reduce-scatter.1
where the time goes:
time: 410 us; the launch traced here: 409 us
  waiting for transfers between devices  320 us (78%)
  matrix products  28.9 us (7%)
  blocking collectives  17.8 us (4%)
  starting transfers between devices  16.7 us (4%)
  between operations  14.1 us (3%)
  other arithmetic  6.2 us (2%)
  local copies, waits for them, and re-layouts  5.5 us (1%)
    reduce_scatter x1, waiting for transfers between devices, body(): lax.psum_scatter(image_terms, 'dp', scatter_dimension=0, tiled=True)  183 us
    all_gather x1, waiting for transfers between devices, body(): piece = lax.all_gather(images_wide, 'dp', axis=0, tiled=True)  114 us
    dot_general x1, matrix products, cross_rows(): lax.dot_general(left, right, (((1,), (1,)), ((), ())), preferred_element_...  13.1 us
    all_to_all x1, waiting for transfers between devices, body(): lax.all_to_all(text_total.astype(jnp.bfloat16), 'dp', split_axis=0, conca...  11.8 us
    all_to_all x1, waiting for transfers between devices, body(): lax.all_to_all(outgoing, 'dp', split_axis=0, concat_axis=0, tiled=True)  11.4 us
    all_to_all x1, starting transfers between devices, body(): lax.all_to_all(outgoing, 'dp', split_axis=0, concat_axis=0, tiled=True)  11.1 us
    all_gather x1, blocking collectives, body(): lax.all_gather(owned_rows, 'mp', axis=1, tiled=True)  9.74 us
  transfers between devices with their start and end apart: 4, of which 4 were waited for; matrix products, arithmetic and copies ran while one was open for 3% of the time, Pallas kernels for 0%

commit v1 on v0

--- a/solution.py
+++ b/solution.py
@@ -55,7 +55,9 @@
     slot_global = jnp.where(pair_image >= 0, holder * image_count + pair_image, -1)
     own_positive = (pair_image[None, :] == local_rows[:, None]).astype(jnp.float32)
     slot_inverse = jnp.sum(own_positive * inverse_count[:, None], axis=0)
-    piece = lax.all_gather(images_wide, "dp", axis=0, tiled=True)
+    piece = jnp.concatenate(
+        lax.all_to_all(jnp.stack([images_wide] * lax.axis_size("dp")), "dp", 0, 0), axis=0
+    )
     count = piece.shape[0]
     piece_rows = jnp.arange(count, dtype=jnp.int32)
     positive = (piece_rows[:, None] == slot_global[None, :]).astype(jnp.float32)

time: 410 us -> 579 us (1.41)
  blocking collectives: 17.8 us -> 272 us
  waiting for transfers between devices: 320 us -> 194 us
  starting transfers between devices: 16.7 us -> 45.6 us
  local copies, waits for them, and re-layouts: 5.5 us -> 12.9 us
  matrix products: 28.9 us -> 34.9 us
    all_gather x1, blocking collectives: 9.74 us -> 264 us  [body(): lax.all_gather(owned_rows, 'mp', axis=1, tiled=True)]
    all_gather x1 -> x0, waiting for transfers between devices: 114 us -> none  [body(): piece = lax.all_gather(images_wide, 'dp', axis=0, tiled=True)]
    all_to_all x1, starting transfers between devices: 5.5 us -> 26.1 us  [body(): lax.all_to_all(text_total.astype(jnp.bfloat16), 'dp', split_axis=0, conca...]
    all_to_all x0 -> x1, starting transfers between devices: none -> 7.91 us  [body(): lax.all_to_all(jnp.stack([images_wide] * lax.axis_size('dp')), 'dp', 0, 0)]
    all_to_all x1, waiting for transfers between devices: 11.4 us -> 3.61 us  [body(): lax.all_to_all(outgoing, 'dp', split_axis=0, concat_axis=0, tiled=True)]
    another operation x0 -> x1, local copies, waits for them, and re-layouts: none -> 7.17 us  [body(): jnp.stack([images_wide] * lax.axis_size('dp'))]
    dot_general x1, matrix products: 7.59 us -> 14.3 us  [down_rows(): lax.dot_general(left, right, (((0,), (0,)), ((), ())), preferred_element_...]
  transfers between devices with their start and end apart: 4 -> 4, of which waited for: 4 -> 3; matrix products, arithmetic and copies ran while one was open for 3% -> 3% of each run, Pallas kernels for 0% -> 0%
where the time goes in v1:
time: 579 us
  blocking collectives  272 us (47%)
  waiting for transfers between devices  194 us (34%)
  starting transfers between devices  45.6 us (8%)
  matrix products  34.9 us (6%)
  between operations  14.2 us (2%)
  local copies, waits for them, and re-layouts  12.9 us (2%)
    all_gather x1, blocking collectives, body(): lax.all_gather(owned_rows, 'mp', axis=1, tiled=True)  264 us
    reduce_scatter x1, waiting for transfers between devices, body(): lax.psum_scatter(image_terms, 'dp', scatter_dimension=0, tiled=True)  179 us
    all_to_all x1, starting transfers between devices, body(): lax.all_to_all(text_total.astype(jnp.bfloat16), 'dp', split_axis=0, conca...  26.1 us
    dot_general x1, matrix products, down_rows(): lax.dot_general(left, right, (((0,), (0,)), ((), ())), preferred_element_...  14.3 us
    dot_general x1, matrix products, cross_rows(): lax.dot_general(left, right, (((1,), (1,)), ((), ())), preferred_element_...  12.4 us
    all_to_all x1, waiting for transfers between devices, body(): lax.all_to_all(text_total.astype(jnp.bfloat16), 'dp', split_axis=0, conca...  11.8 us
  transfers between devices with their start and end apart: 4, of which 3 were waited for; matrix products, arithmetic and copies ran while one was open for 3% of the time, Pallas kernels for 0%

profile of v1, /device:TPU:0, one launch (start us, length us, event | category | flops | bytes accessed | tf_op | source)
XLA Modules:
  0.0 578.5 jit_solution(15226270923576821229)
XLA Ops:
  7.2 0.0 copy-start
  7.2 0.9 convert_reduce_fusion
  8.1 0.7 compare_and_fusion
  8.8 0.0 copy-done
  8.8 0.3 convolution_convert_fusion
  9.1 0.2 copy.16
  9.3 0.8 all_to_all.19
  10.1 11.5 %all-to-all-start = ((bf16[64,4,576]{2,1,0:T(4,128)(2,1)}), bf16[64,4,576]{2,1,0:T(4,128)(2,1)S(1)}, u32[]{:S(2)}, u32[]{:S(2)}) async-start(bf16[64,4,576]{2,1,0:T(4,128)(2,1)} %all_to_all.19), calls=%async_computation | async-start | bytes 655360 | tf_op jit(solution)/shard_map/all_to_all | solution.py:48
  21.6 8.0 %all_gather.7 = bf16[128,1152]{0,1:T(8,128)(2,1)S(1)} all-gather(bf16[128,576]{0,1:T(8,128)(2,1)} %param.5), channel_id=1, replica_groups=mesh['dp'=64,'mp'=2] {'mp'}, dimensions={1}, use_global_device_ids=true | all-gather | bytes 442368 | tf_op jit(solution)/shard_map/all_gather | solution.py:50
  29.7 0.2 copy.18
  29.9 3.6 all-to-all-done
  33.5 7.2 %stack.2 = bf16[64,128,1152]{2,1,0:T(8,128)(2,1)} broadcast(bf16[128,1152]{1,0:T(8,128)(2,1)S(1)} %copy.18), dimensions={1,2} | broadcast | bytes 19169280 | tf_op jit(solution)/shard_map/stack | solution.py:59
  40.6 0.0 copy-start.3
  40.6 0.0 copy-start.2
  40.6 7.9 %all-to-all-start.1 = ((bf16[64,128,1152]{2,1,0:T(8,128)(2,1)}), bf16[64,128,1152]{2,1,0:T(8,128)(2,1)}, u32[]{:S(2)}, u32[]{:S(2)}) async-start(bf16[64,128,1152]{2,1,0:T(8,128)(2,1)} %stack.2), calls=%async_computation.1 | async-start | bytes 37748736 | tf_op jit(solution)/shard_map/all_to_all | solution.py:59
  48.6 0.0 reduce-scatter.2.cloned.1.call-start
  48.6 0.0 copy-done.3
  48.6 0.0 copy-done.2
  48.7 0.1 select_reduce_fusion
  48.8 0.2 all_to_all.21
  48.9 0.2 copy.17
  49.1 264.4 %all_gather.6 = bf16[256,1152]{0,1:T(8,128)(2,1)S(1)} all-gather(bf16[256,576]{0,1:T(8,128)(2,1)S(1)} %copy.17), channel_id=1, replica_groups=mesh['dp'=64,'mp'=2] {'mp'}, dimensions={1}, use_global_device_ids=true | all-gather | bytes 884736 | tf_op jit(solution)/shard_map/all_gather | solution.py:51
  313.5 0.0 all-to-all-done.1
  313.5 12.4 %fusion.10 = bf16[8192,256]{0,1:T(8,128)(2,1)S(1)} fusion(bf16[256,1152]{0,1:T(8,128)(2,1)S(1)} %all_gather.6, bf16[8192,1152]{1,0:T(8,128)(2,1)} %bitcast, f32[256]{0:T(256)S(1)} %broadcast_add_fusion, s32[256]{0:T(256)S(1)} %compare_select_fusion.1), kind=kOutput, calls=%fused_computation.12 | convolution fusion | flops 4859101184 | bytes 23660544 | tf_op jit(solution)/shard_map/dot_general | solution.py:11
  326.0 0.0 copy-start.1
  326.0 1.9 copy-done.1
  327.9 7.9 %fusion.17 = f32[8192,576]{0,1:T(8,128)} fusion(bf16[8192,256]{0,1:T(8,128)(2,1)S(1)} %fusion.10, bf16[256,576]{1,0:T(8,128)(2,1)S(1)} %all_to_all.21), kind=kOutput, calls=%fused_computation.32 | convolution fusion | flops 2415919104 | bytes 23363584 | tf_op jit(solution)/shard_map/dot_general | solution.py:69
  335.8 0.0 reduce-scatter.2.cloned.1.call-update
  335.8 14.3 %fusion.11 = bf16[256,576]{0,1:T(8,128)(2,1)S(1)} fusion(bf16[8192,256]{0,1:T(8,128)(2,1)} %copy-done.1, bf16[8192,1152]{1,0:T(8,128)(2,1)} %bitcast, s32[]{:T(128)S(6)} %select_n.18), kind=kOutput, calls=%fused_computation.15 | convolution fusion | flops 2416066560 | bytes 14974980 | tf_op jit(solution)/shard_map/dot_general | solution.py:17
  350.1 0.2 copy.19
  350.3 0.8 all_to_all.23
  351.1 26.1 %all-to-all-start.2 = ((bf16[64,4,576]{2,1,0:T(4,128)(2,1)}), bf16[64,4,576]{2,1,0:T(4,128)(2,1)S(1)}, u32[]{:S(2)}, u32[]{:S(2)}) async-start(bf16[64,4,576]{2,1,0:T(4,128)(2,1)} %all_to_all.23), calls=%async_computation.3 | async-start | bytes 655360 | tf_op jit(solution)/shard_map/all_to_all | solution.py:72
  377.3 11.8 %all-to-all-done.2 = bf16[64,4,576]{2,1,0:T(4,128)(2,1)S(1)} async-done(((bf16[64,4,576]{2,1,0:T(4,128)(2,1)}), bf16[64,4,576]{2,1,0:T(4,128)(2,1)S(1)}, u32[]{:S(2)}, u32[]{:S(2)}) %all-to-all-start.2) | async-done | bytes 294944 | tf_op jit(solution)/shard_map/all_to_all | solution.py:72
  389.0 0.2 all_to_all.25
  389.2 1.0 gather_fusion
  390.2 0.8 broadcast_select_fusion
  391.0 179.0 %reduce-scatter.2.cloned.1.call-done = f32[128,576]{0,1:T(8,128)} async-done(((f32[8192,576]{0,1:T(8,128)}), f32[128,576]{0,1:T(8,128)}) %reduce-scatter.2.cloned.1.call-update) | async-done | bytes 294928 | tf_op jit(solution)/shard_map/reduce_scatter | solution.py:71
  570.0 1.6 convert_element_type.28
  (5 shorter events, 0.0 us)
Async XLA Ops:
  7.2 1.7 copy-start
  10.1 23.3 %all-to-all-start = ((bf16[64,4,576]{2,1,0:T(4,128)(2,1)}), bf16[64,4,576]{2,1,0:T(4,128)(2,1)S(1)}, u32[]{:S(2)}, u32[]{:S(2)}) async-start(bf16[64,4,576]{2,1,0:T(4,128)(2,1)} %all_to_all.19), calls=%async_computation | async-start | bytes 655360 | tf_op jit(solution)/shard_map/all_to_all | solution.py:48
  40.6 8.0 %copy-start.3 = (s32[128]{0:T(128)S(1)}, s32[128]{0:T(128)}, u32[]{:S(2)}) copy-start(s32[128]{0:T(128)} %param.7) | copy-start | bytes 1540
  40.6 8.0 %copy-start.2 = (s32[256]{0:T(256)S(1)}, s32[256]{0:T(256)}, u32[]{:S(2)}) copy-start(s32[256]{0:T(256)} %param.9) | copy-start | bytes 3076
  40.6 272.9 %all-to-all-start.1 = ((bf16[64,128,1152]{2,1,0:T(8,128)(2,1)}), bf16[64,128,1152]{2,1,0:T(8,128)(2,1)}, u32[]{:S(2)}, u32[]{:S(2)}) async-start(bf16[64,128,1152]{2,1,0:T(8,128)(2,1)} %stack.2), calls=%async_computation.1 | async-start | bytes 37748736 | tf_op jit(solution)/shard_map/all_to_all | solution.py:59
  48.6 521.5 %reduce-scatter.2.cloned.1.call-start = ((), (), s32[]{:S(2)}) async-start(), calls=%async_computation.4 | async-start | bytes 19169280 | tf_op jit(solution)/shard_map/reduce_scatter | solution.py:71
  326.0 2.0 copy-start.1
  351.1 37.9 %all-to-all-start.2 = ((bf16[64,4,576]{2,1,0:T(4,128)(2,1)}), bf16[64,4,576]{2,1,0:T(4,128)(2,1)S(1)}, u32[]{:S(2)}, u32[]{:S(2)}) async-start(bf16[64,4,576]{2,1,0:T(4,128)(2,1)} %all_to_all.23), calls=%async_computation.3 | async-start | bytes 655360 | tf_op jit(solution)/shard_map/all_to_all | solution.py:72
Sparse Core Ops, SparseCore 0:
  336.0 234.0 reduce-scatter.1
